TPU v7x, 32 devices: a whole 2x2x4 slice. The times are simulated.
32 devices in a mesh: dp: 4 (over z), fsdp: 2 (over x), expert: 4 (over y, core).
Axes of the slice: x: 2, y: 2, z: 4, core: 2. Of those that a mesh axis runs over, the one named last changes fastest.
Arguments:
- tokens: bfloat16 [2048, 4096], P(('dp', 'expert'), 'fsdp'), may hold values from -6 to 6
- cotangent: bfloat16 [2048, 4096], P(('dp', 'expert'), 'fsdp'), may hold values from -6 to 6
- routes: int32 [2048, 8], P(('dp', 'expert')), may hold values from 0 to 127, as said below
- route_gates: float32 [2048, 8], P(('dp', 'expert')), may hold values from 0.05 to 0.6
- gate_weight: bfloat16 [4, 4096, 768], P('expert', None, 'fsdp'), may hold values from -0.09375 to 0.09375
- up_weight: bfloat16 [4, 4096, 768], P('expert', None, 'fsdp'), may hold values from -0.09375 to 0.09375
- down_weight: bfloat16 [4, 768, 4096], P('expert', 'fsdp'), may hold values from -0.21875 to 0.21875
Outputs:
- token_grads: bfloat16 [2048, 4096], P(('dp', 'expert'), 'fsdp')
- gate_grads: bfloat16 [4, 4096, 768], P('expert', 'dp', 'fsdp')
- up_grads: bfloat16 [4, 4096, 768], P('expert', 'dp', 'fsdp')
- down_grads: bfloat16 [4, 768, 4096], P('expert', 'fsdp', 'dp')
Inputs may be any that keep to these rules, and one draw needn't show every extreme that they name: `routes`: each token names 8 different ids, exactly one in each run of 16 ids (0 to 15, 16 to 31, and so on). In each aligned block of 128 tokens (one index of dp and expert together) no id below 16 is named by more than 10 tokens, and in every draw one id below 4 is named by exactly 10 tokens of every block.
All inputs are finite; a program needn't handle non-finite values.
Results may differ from a plain program's by a relative error of at most 0.017.
Values may be sent and summed in bfloat16 or wider, within the bound.
A program may use at most 64 MiB of HBM per device.

v0:
```python
import jax
import jax.numpy as jnp
from jax import lax
from jax.sharding import PartitionSpec as P

CAP = 10


def local(tokens, cotangent, routes, route_gates, gate_weight, up_weight, down_weight):
    owners = lax.axis_size("expert")
    quarter = tokens.shape[1]
    in_window = routes < owners
    target = jnp.where(
        jnp.any(in_window, axis=1), jnp.sum(jnp.where(in_window, routes, 0), axis=1), owners
    )
    route_gate = jnp.sum(jnp.where(in_window, route_gates, jnp.float32(0.0)), axis=1)
    scaled = (route_gate[:, None] * cotangent.astype(jnp.float32)).astype(jnp.bfloat16)
    onehot = (target[:, None] == jnp.arange(owners, dtype=jnp.int32)[None, :]).astype(jnp.int32)
    before = jnp.cumsum(onehot, axis=0) - onehot
    position = target * CAP + jnp.sum(before * onehot, axis=1)
    slot_count = owners * CAP
    selector = (jnp.arange(slot_count, dtype=jnp.int32)[:, None] == position[None, :]).astype(
        jnp.bfloat16
    )
    send_rows = (
        jnp.dot(selector, tokens, preferred_element_type=jnp.float32)
        .astype(jnp.bfloat16)
        .reshape(owners, CAP, quarter)
    )
    send_grads = (
        jnp.dot(selector, scaled, preferred_element_type=jnp.float32)
        .astype(jnp.bfloat16)
        .reshape(owners, CAP, quarter)
    )
    recv_rows, recv_grads = (
        lax.all_to_all(send_rows, "expert", split_axis=0, concat_axis=0, tiled=True),
        lax.all_to_all(send_grads, "expert", split_axis=0, concat_axis=0, tiled=True),
    )
    flat_rows = recv_rows.reshape(slot_count, quarter)
    flat_grads = recv_grads.reshape(slot_count, quarter)
    full_rows, full_grads = (
        lax.all_gather(flat_rows, "fsdp", axis=1, tiled=True),
        lax.all_gather(flat_grads, "fsdp", axis=1, tiled=True),
    )
    gate_mat = gate_weight[0]
    up_mat = up_weight[0]
    down_mat = down_weight[0]
    across = (((1,), (1,)), ((), ()))
    gate_pre = jnp.dot(full_rows, gate_mat, preferred_element_type=jnp.float32)
    up_pre = jnp.dot(full_rows, up_mat, preferred_element_type=jnp.float32)
    sigmoid_gate = jax.nn.sigmoid(gate_pre)
    activated = gate_pre * sigmoid_gate
    hidden = (activated * up_pre).astype(jnp.bfloat16)
    hidden_grad = lax.dot_general(full_grads, down_mat, across, preferred_element_type=jnp.float32)
    gate_grad = (
        hidden_grad * up_pre * sigmoid_gate * (1.0 + gate_pre * (1.0 - sigmoid_gate))
    ).astype(jnp.bfloat16)
    up_grad = (hidden_grad * activated).astype(jnp.bfloat16)
    partial_value = lax.dot_general(gate_grad, gate_mat, across, preferred_element_type=jnp.float32)
    partial_value = partial_value + lax.dot_general(
        up_grad, up_mat, across, preferred_element_type=jnp.float32
    )
    route_rows = lax.psum_scatter(
        partial_value.astype(jnp.bfloat16), "fsdp", scatter_dimension=1, tiled=True
    )
    returned = lax.all_to_all(
        route_rows.reshape(owners, CAP, quarter), "expert", split_axis=0, concat_axis=0, tiled=True
    )
    token_grads = lax.dot_general(
        selector,
        returned.reshape(slot_count, quarter),
        (((0,), (0,)), ((), ())),
        preferred_element_type=jnp.float32,
    ).astype(jnp.bfloat16)
    block_width = gate_mat.shape[1]
    contract = (((0,), (0,)), ((), ()))
    summed = lax.psum_scatter(
        jnp.concatenate(
            [
                lax.dot_general(full_rows, gate_grad, contract, preferred_element_type=jnp.float32),
                lax.dot_general(full_rows, up_grad, contract, preferred_element_type=jnp.float32),
                lax.dot_general(full_grads, hidden, contract, preferred_element_type=jnp.float32),
            ],
            axis=1,
        ).astype(jnp.bfloat16),
        "dp",
        scatter_dimension=0,
        tiled=True,
    ).astype(jnp.float32)
    gate_grads = summed[:, :block_width].astype(jnp.bfloat16)[None]
    up_grads = summed[:, block_width : 2 * block_width].astype(jnp.bfloat16)[None]
    down_grads = summed[:, 2 * block_width :].astype(jnp.bfloat16).T[None]
    return (token_grads, gate_grads, up_grads, down_grads)


def solution(mesh):
    placed = (
        P(("dp", "expert"), "fsdp"),
        P(("dp", "expert"), "fsdp"),
        P(("dp", "expert"), None),
        P(("dp", "expert"), None),
        P("expert", None, "fsdp"),
        P("expert", None, "fsdp"),
        P("expert", "fsdp", None),
    )
    return jax.shard_map(
        local,
        mesh=mesh,
        in_specs=placed,
        out_specs=(
            P(("dp", "expert"), "fsdp"),
            P("expert", "dp", "fsdp"),
            P("expert", "dp", "fsdp"),
            P("expert", "fsdp", "dp"),
        ),
        check_vma=False,
    )
```

profile of v0, /device:TPU:8, one launch (start us, length us, event | category | flops | bytes accessed | tf_op | source)
XLA Modules:
  0.0 248.2 jit_solution(13827624348237220745)
XLA Ops:
  7.2 0.0 copy-start
  7.2 0.9 fusion.18
  8.0 0.8 select_reduce_fusion.2
  8.8 0.1 fusion.11
  8.9 0.2 reduce_window_sum.11
  9.1 0.2 select_reduce_fusion
  9.3 1.2 convolution_convert_fusion.4
  10.6 0.8 reshape.43
  11.3 3.4 %all-to-all-start.1 = ((bf16[4,10,2048]{2,1,0:T(8,128)(2,1)}), bf16[4,10,2048]{2,1,0:T(8,128)(2,1)S(1)}, u32[]{:S(2)}, u32[]{:S(2)}) async-start(bf16[4,10,2048]{2,1,0:T(8,128)(2,1)} %reshape.43), calls=%async_computation.1 | async-start | bytes 524288 | tf_op jit(solution)/shard_map/all_to_all | solution.py:36
  14.7 0.7 select_reduce_fusion.1
  15.4 2.0 convolution_convert_fusion.5
  17.4 1.7 reshape.41
  19.1 1.6 all-to-all-done.1
  20.7 4.0 %all-to-all-start = ((bf16[4,10,2048]{2,1,0:T(8,128)(2,1)}), bf16[4,10,2048]{2,1,0:T(8,128)(2,1)}, u32[]{:S(2)}, u32[]{:S(2)}) async-start(bf16[4,10,2048]{2,1,0:T(8,128)(2,1)} %reshape.41), calls=%async_computation | async-start | bytes 524288 | tf_op jit(solution)/shard_map/all_to_all | solution.py:37
  24.8 0.0 reduce-scatter.3.cloned.1.call-start
  24.8 0.7 reshape.44
  25.6 0.0 copy-start.1
  25.6 7.5 %all_gather.7 = bf16[40,4096]{1,0:T(8,128)(2,1)S(1)} all-gather(bf16[40,2048]{1,0:T(8,128)(2,1)} %reshape.44), channel_id=1, replica_groups=mesh['dp'=4,'fsdp'=2,'expert'=4] {'fsdp'}, dimensions={1}, use_global_device_ids=true | all-gather | bytes 491520 | tf_op jit(solution)/shard_map/all_gather | solution.py:42
  33.1 0.0 copy-done
  33.1 0.6 fusion.3
  33.7 0.0 copy-done.1
  33.7 1.2 fusion.6
  34.9 0.0 all-to-all-done
  34.9 1.7 reshape.42
  36.5 0.0 copy-start.3
  36.5 0.0 copy-start.4
  36.5 6.8 %all_gather.6 = bf16[40,4096]{1,0:T(8,128)(2,1)S(1)} all-gather(bf16[40,2048]{1,0:T(8,128)(2,1)} %reshape.42), channel_id=1, replica_groups=mesh['dp'=4,'fsdp'=2,'expert'=4] {'fsdp'}, dimensions={1}, use_global_device_ids=true | all-gather | bytes 491520 | tf_op jit(solution)/shard_map/all_gather | solution.py:43
  43.3 3.5 %convolution_convert_fusion = bf16[4096,384]{0,1:T(8,128)(2,1)} fusion(bf16[40,4096]{1,0:T(8,128)(2,1)S(1)} %all_gather.6, f32[40,384]{1,0:T(8,128)} %fusion.6, f32[40,384]{1,0:T(8,128)S(1)} %fusion.3), kind=kOutput, calls=%fused_computation.1 | convolution fusion | flops 127494144 | bytes 3596288 | tf_op jit(solution)/shard_map/dot_general | solution.py:82
  46.8 0.0 copy-done.3
  46.8 0.0 copy-done.4
  46.8 1.0 multiply_convert_fusion.3
  47.9 2.7 %convolution_convert_fusion.2 = bf16[4096,384]{0,1:T(8,128)(2,1)} fusion(bf16[40,4096]{1,0:T(8,128)(2,1)S(1)} %all_gather.7, bf16[40,384]{1,0:T(8,128)(2,1)S(1)} %get-tuple-element.16), kind=kOutput, calls=%fused_computation.3 | convolution fusion | flops 127401984 | bytes 3504128 | tf_op jit(solution)/shard_map/dot_general | solution.py:80
  50.5 0.0 copy-start.2
  50.5 1.3 fusion.1
  51.9 2.7 %convolution_convert_fusion.1 = bf16[4096,384]{0,1:T(8,128)(2,1)} fusion(bf16[40,4096]{1,0:T(8,128)(2,1)S(1)} %all_gather.7, bf16[40,384]{1,0:T(8,128)(2,1)S(1)} %get-tuple-element.15), kind=kOutput, calls=%fused_computation.2 | convolution fusion | flops 127401984 | bytes 3504128 | tf_op jit(solution)/shard_map/dot_general | solution.py:81
  54.6 0.0 copy-done.2
  54.6 2.1 fusion
  56.6 0.0 reduce-scatter.3.cloned.1.call-update
  56.7 0.0 reduce-scatter.5.cloned.1.call-start
  56.7 7.8 %pad_maximum_fusion = bf16[4096,1152]{0,1:T(8,128)(2,1)} fusion(bf16[4096,384]{0,1:T(8,128)(2,1)} %convolution_convert_fusion, bf16[4096,384]{0,1:T(8,128)(2,1)} %convolution_convert_fusion.1, bf16[4096,384]{0,1:T(8,128)(2,1)} %convolution_convert_fusion.2), kind=kLoop, calls=%fused_computation | loop fusion | flops 28311552 | bytes 18874368 | tf_op jit(solution)/shard_map/concatenate | solution.py:78
  64.5 0.0 reduce-scatter.5.cloned.1.call-update
  64.5 5.7 %reduce-scatter.3.cloned.1.call-done = bf16[40,2048]{1,0:T(8,128)(2,1)} async-done(((bf16[40,4096]{1,0:T(8,128)(2,1)}), bf16[40,2048]{1,0:T(8,128)(2,1)}) %reduce-scatter.3.cloned.1.call-update) | async-done | bytes 163856 | tf_op jit(solution)/shard_map/reduce_scatter | solution.py:63
  70.2 1.0 reshape.45
  71.1 9.1 %all_to_all.15 = bf16[4,10,2048]{2,1,0:T(8,128)(2,1)} all-to-all(bf16[4,10,2048]{2,1,0:T(8,128)(2,1)S(1)} %reshape.45), channel_id=1, replica_groups=mesh['dp'=4,'fsdp'=2,'expert'=4] {'expert'}, dimensions={0} | all-to-all | bytes 327680 | tf_op jit(solution)/shard_map/all_to_all | solution.py:66
  80.2 1.0 reshape.46
  81.2 1.1 convolution_convert_fusion.3
  82.4 151.4 %reduce-scatter.5.cloned.1.call-done = bf16[1024,1152]{0,1:T(8,128)(2,1)} async-done(((bf16[4096,1152]{0,1:T(8,128)(2,1)}), bf16[1024,1152]{0,1:T(8,128)(2,1)}) %reduce-scatter.5.cloned.1.call-update) | async-done | bytes 2359312 | tf_op jit(solution)/shard_map/reduce_scatter | solution.py:77
  233.8 3.1 %slice_bitcast_fusion = (bf16[1,384,1024]{2,1,0:T(8,128)(2,1)}, bf16[1,1024,384]{1,2,0:T(8,128)(2,1)}, bf16[1,1024,384]{1,2,0:T(8,128)(2,1)}) fusion(bf16[1024,1152]{0,1:T(8,128)(2,1)} %reduce-scatter.5.cloned.1.call-done), kind=kLoop, calls=%fused_computation.19 | loop fusion | bytes 4718592 | tf_op jit(solution)/shard_map/broadcast_in_dim | solution.py:92
  236.8 2.3 copy.13
  239.1 2.3 copy.14
  (2 shorter events, 0.0 us)
Async XLA Ops:
  7.2 25.9 %copy-start = (bf16[1,4096,384]{2,1,0:T(8,128)(2,1)S(1)}, bf16[1,4096,384]{2,1,0:T(8,128)(2,1)}, u32[]{:S(2)}) copy-start(bf16[1,4096,384]{2,1,0:T(8,128)(2,1)} %param.11) | copy-start | bytes 9437188
  11.3 9.4 %all-to-all-start.1 = ((bf16[4,10,2048]{2,1,0:T(8,128)(2,1)}), bf16[4,10,2048]{2,1,0:T(8,128)(2,1)S(1)}, u32[]{:S(2)}, u32[]{:S(2)}) async-start(bf16[4,10,2048]{2,1,0:T(8,128)(2,1)} %reshape.43), calls=%async_computation.1 | async-start | bytes 524288 | tf_op jit(solution)/shard_map/all_to_all | solution.py:36
  20.7 14.1 %all-to-all-start = ((bf16[4,10,2048]{2,1,0:T(8,128)(2,1)}), bf16[4,10,2048]{2,1,0:T(8,128)(2,1)}, u32[]{:S(2)}, u32[]{:S(2)}) async-start(bf16[4,10,2048]{2,1,0:T(8,128)(2,1)} %reshape.41), calls=%async_computation | async-start | bytes 524288 | tf_op jit(solution)/shard_map/all_to_all | solution.py:37
  24.8 45.4 %reduce-scatter.3.cloned.1.call-start = ((), (), s32[]{:S(2)}) async-start(), calls=%async_computation.5 | async-start | bytes 491520 | tf_op jit(solution)/shard_map/reduce_scatter | solution.py:63
  25.6 8.1 %copy-start.1 = (bf16[1,4096,384]{2,1,0:T(8,128)(2,1)S(1)}, bf16[1,4096,384]{2,1,0:T(8,128)(2,1)}, u32[]{:S(2)}) copy-start(bf16[1,4096,384]{2,1,0:T(8,128)(2,1)} %param.12) | copy-start | bytes 9437188
  36.5 10.3 %copy-start.3 = (bf16[1,384,4096]{2,1,0:T(8,128)(2,1)S(1)}, bf16[1,384,4096]{2,1,0:T(8,128)(2,1)}, u32[]{:S(2)}) copy-start(bf16[1,384,4096]{2,1,0:T(8,128)(2,1)} %param.13) | copy-start | bytes 9437188
  36.5 10.3 %copy-start.4 = (f32[40,384]{1,0:T(8,128)S(1)}, f32[40,384]{1,0:T(8,128)}, u32[]{:S(2)}) copy-start(f32[40,384]{1,0:T(8,128)} %fusion.6) | copy-start | bytes 184324
  50.5 4.0 %copy-start.2 = (bf16[1,4096,384]{2,1,0:T(8,128)(2,1)S(1)}, bf16[1,4096,384]{2,1,0:T(8,128)(2,1)}, u32[]{:S(2)}) copy-start(bf16[1,4096,384]{2,1,0:T(8,128)(2,1)} %param.12) | copy-start | bytes 9437188
  56.7 177.1 %reduce-scatter.5.cloned.1.call-start = ((), (), s32[]{:S(2)}) async-start(), calls=%async_computation.6 | async-start | bytes 11796480 | tf_op jit(solution)/shard_map/reduce_scatter | solution.py:77
Sparse Core Ops, SparseCore 0:
  56.8 13.3 reduce-scatter.2
  72.6 161.0 reduce-scatter.4
where the time goes:
time: 251 us; the launch traced here: 248 us
  waiting for transfers between devices  159 us (63%)
  blocking collectives  23.4 us (9%)
  matrix products  19.4 us (8%)
  local copies, waits for them, and re-layouts  14.5 us (6%)
  between operations  14.1 us (6%)
  other arithmetic  10.6 us (4%)
  starting transfers between devices  7.53 us (3%)
    reduce_scatter x1, waiting for transfers between devices, local(): lax.psum_scatter(jnp.concatenate([lax.dot_general(full_rows, gate_grad, c...  151 us
    all_to_all x1, blocking collectives, local(): lax.all_to_all(route_rows.reshape(owners, CAP, quarter), 'expert', split_...  9.08 us
    concatenate x1, other arithmetic, local(): jnp.concatenate([lax.dot_general(full_rows, gate_grad, contract, preferre...  7.75 us
    all_gather x1, blocking collectives, local(): lax.all_gather(flat_rows, 'fsdp', axis=1, tiled=True)  7.55 us
    all_gather x1, blocking collectives, local(): lax.all_gather(flat_grads, 'fsdp', axis=1, tiled=True)  6.75 us
    reduce_scatter x1, waiting for transfers between devices, local(): lax.psum_scatter(partial_value.astype(jnp.bfloat16), 'fsdp', scatter_dime...  5.67 us
  transfers between devices with their start and end apart: 4, of which 3 were waited for; matrix products, arithmetic and copies ran while one was open for 7% of the time, Pallas kernels for 0%

commit v1 on v0

--- a/solution.py
+++ b/solution.py
@@ -72,24 +72,29 @@
         (((0,), (0,)), ((), ())),
         preferred_element_type=jnp.float32,
     ).astype(jnp.bfloat16)
+    contract = (((0,), (0,)), ((), ()))
     block_width = gate_mat.shape[1]
-    contract = (((0,), (0,)), ((), ()))
-    summed = lax.psum_scatter(
-        jnp.concatenate(
-            [
-                lax.dot_general(full_rows, gate_grad, contract, preferred_element_type=jnp.float32),
-                lax.dot_general(full_rows, up_grad, contract, preferred_element_type=jnp.float32),
-                lax.dot_general(full_grads, hidden, contract, preferred_element_type=jnp.float32),
-            ],
-            axis=1,
-        ).astype(jnp.bfloat16),
-        "dp",
-        scatter_dimension=0,
-        tiled=True,
-    ).astype(jnp.float32)
-    gate_grads = summed[:, :block_width].astype(jnp.bfloat16)[None]
-    up_grads = summed[:, block_width : 2 * block_width].astype(jnp.bfloat16)[None]
-    down_grads = summed[:, 2 * block_width :].astype(jnp.bfloat16).T[None]
+    groups = lax.axis_size("dp")
+    slices = jnp.concatenate([full_rows, full_grads], axis=0).reshape(
+        2 * slot_count, groups, -1
+    )
+    slices = lax.all_to_all(slices, "dp", split_axis=1, concat_axis=1, tiled=True)
+    slices = slices.reshape(2, slot_count, groups, -1)
+    factors = lax.all_gather(
+        jnp.concatenate([gate_grad, up_grad, hidden], axis=1), "dp", axis=1, tiled=False
+    )
+    many = slot_count * groups
+    rows_slice = slices[0].reshape(many, -1)
+    grads_slice = slices[1].reshape(many, -1)
+    factors = factors.reshape(many, -1)
+    gate_up = lax.dot_general(
+        rows_slice, factors[:, : 2 * block_width], contract, preferred_element_type=jnp.float32
+    ).astype(jnp.bfloat16)
+    gate_grads = gate_up[:, :block_width][None]
+    up_grads = gate_up[:, block_width:][None]
+    down_grads = lax.dot_general(
+        factors[:, 2 * block_width :], grads_slice, contract, preferred_element_type=jnp.float32
+    ).astype(jnp.bfloat16)[None]
     return (token_grads, gate_grads, up_grads, down_grads)
 
 

time: 251 us -> 133 us (0.53)
  waiting for transfers between devices: 159 us -> 19.3 us
  blocking collectives: 23.4 us -> 38.3 us
  starting transfers between devices: 7.53 us -> 16.7 us
  other arithmetic: 10.6 us -> 4.59 us
  local copies, waits for them, and re-layouts: 14.5 us -> 19.7 us
    reduce_scatter x1 -> x0, waiting for transfers between devices: 151 us -> none  [local(): lax.psum_scatter(jnp.concatenate([lax.dot_general(full_rows, gate_grad, c...]
    all_gather x0 -> x1, blocking collectives: none -> 24.2 us  [local(): lax.all_gather(jnp.concatenate([gate_grad, up_grad, hidden], axis=1), 'dp...]
    all_to_all x0 -> x2, starting transfers between devices: none -> 9.19 us  [the longest x1 5.14 us: local(): lax.all_to_all(slices, 'dp', split_axis=1, concat_axis=1, tiled=True)]
    all_to_all x1 -> x0, blocking collectives: 9.08 us -> none  [local(): lax.all_to_all(route_rows.reshape(owners, CAP, quarter), 'expert', split_...]
    reduce_scatter x1, waiting for transfers between devices: 5.67 us -> 13.5 us  [local(): lax.psum_scatter(partial_value.astype(jnp.bfloat16), 'fsdp', scatter_dime...]
    concatenate x1 -> x2, other arithmetic: 7.75 us -> 1.78 us  [the longest x1 1.02 us: local(): jnp.concatenate([full_rows, full_grads], axis=0)]
    dot_general x3 -> x2, matrix products: 8.89 us -> 3.84 us  [the longest x1 2.25 us: local(): lax.dot_general(factors[:, 2 * block_width:], grads_slice, contract, pref...]
    slice x0 -> x3, local copies, waits for them, and re-layouts: none -> 4.77 us  [the longest x2 2.82 us: local(): grads_slice = slices[1].reshape(many, -1)]
  transfers between devices with their start and end apart: 4 -> 5, of which waited for: 3 -> 3; matrix products, arithmetic and copies ran while one was open for 7% -> 10% of each run, Pallas kernels for 0% -> 0%
where the time goes in v1:
time: 133 us; the launch traced here: 130 us
  blocking collectives  38.3 us (29%)
  local copies, waits for them, and re-layouts  19.7 us (15%)
  waiting for transfers between devices  19.3 us (15%)
  matrix products  17.3 us (13%)
  starting transfers between devices  16.7 us (13%)
  between operations  14.2 us (11%)
  other arithmetic  4.59 us (3%)
    all_gather x1, blocking collectives, local(): lax.all_gather(jnp.concatenate([gate_grad, up_grad, hidden], axis=1), 'dp...  24.2 us
    reduce_scatter x1, waiting for transfers between devices, local(): lax.psum_scatter(partial_value.astype(jnp.bfloat16), 'fsdp', scatter_dime...  13.5 us
    all_gather x1, blocking collectives, local(): lax.all_gather(flat_rows, 'fsdp', axis=1, tiled=True)  7.41 us
    all_gather x1, blocking collectives, local(): lax.all_gather(flat_grads, 'fsdp', axis=1, tiled=True)  6.75 us
    all_to_all x1, starting transfers between devices, local(): lax.all_to_all(slices, 'dp', split_axis=1, concat_axis=1, tiled=True)  5.14 us
    all_to_all x1, waiting for transfers between devices, local(): lax.all_to_all(route_rows.reshape(owners, CAP, quarter), 'expert', split_...  4.19 us
    all_to_all x1, starting transfers between devices, local(): lax.all_to_all(route_rows.reshape(owners, CAP, quarter), 'expert', split_...  4.05 us
    all_to_all x1, starting transfers between devices, local(): lax.all_to_all(send_grads, 'expert', split_axis=0, concat_axis=0, tiled=T...  4.03 us
  transfers between devices with their start and end apart: 5, of which 3 were waited for; matrix products, arithmetic and copies ran while one was open for 10% of the time, Pallas kernels for 0%

profile of v1, /device:TPU:8, one launch (start us, length us, event | category | flops | bytes accessed | tf_op | source)
XLA Modules:
  0.0 130.1 jit_solution(2449130649693223437)
XLA Ops:
  7.2 0.0 copy-start
  7.2 0.9 fusion.19
  8.0 0.8 select_reduce_fusion.2
  8.8 0.1 fusion.14
  8.9 0.2 reduce_window_sum.11
  9.1 0.2 select_reduce_fusion
  9.3 1.2 convolution_convert_fusion.1
  10.6 0.8 reshape.54
  11.3 3.4 %all-to-all-start.1 = ((bf16[4,10,2048]{2,1,0:T(8,128)(2,1)}), bf16[4,10,2048]{2,1,0:T(8,128)(2,1)S(1)}, u32[]{:S(2)}, u32[]{:S(2)}) async-start(bf16[4,10,2048]{2,1,0:T(8,128)(2,1)} %reshape.54), calls=%async_computation.1 | async-start | bytes 524288 | tf_op jit(solution)/shard_map/all_to_all | solution.py:36
  14.7 0.7 select_reduce_fusion.1
  15.4 2.0 %convolution_convert_fusion.2 = bf16[40,2048]{1,0:T(8,128)(2,1)} fusion(bf16[128,2048]{1,0:T(8,128)(2,1)} %param.8, f32[128]{0:T(128)S(1)} %select_reduce_fusion.1, s32[128]{0:T(128)S(1)} %multiply_add_fusion), kind=kOutput, calls=%fused_computation.13 | convolution fusion | flops 21844992 | bytes 689152 | tf_op jit(solution)/shard_map/dot_general | solution.py:31
  17.4 1.7 %reshape.52 = bf16[4,10,2048]{2,1,0:T(8,128)(2,1)} reshape(bf16[40,2048]{1,0:T(8,128)(2,1)} %convolution_convert_fusion.2) | data formatting | bytes 327680 | tf_op jit(solution)/shard_map/reshape | solution.py:33
  19.1 1.6 %all-to-all-done.1 = bf16[4,10,2048]{2,1,0:T(8,128)(2,1)S(1)} async-done(((bf16[4,10,2048]{2,1,0:T(8,128)(2,1)}), bf16[4,10,2048]{2,1,0:T(8,128)(2,1)S(1)}, u32[]{:S(2)}, u32[]{:S(2)}) %all-to-all-start.1) | async-done | bytes 163872 | tf_op jit(solution)/shard_map/all_to_all | solution.py:36
  20.7 4.0 %all-to-all-start = ((bf16[4,10,2048]{2,1,0:T(8,128)(2,1)}), bf16[4,10,2048]{2,1,0:T(8,128)(2,1)}, u32[]{:S(2)}, u32[]{:S(2)}) async-start(bf16[4,10,2048]{2,1,0:T(8,128)(2,1)} %reshape.52), calls=%async_computation | async-start | bytes 524288 | tf_op jit(solution)/shard_map/all_to_all | solution.py:37
  24.8 0.0 reduce-scatter.2.cloned.1.call-start
  24.8 0.7 reshape.55
  25.6 7.4 %all_gather.13 = bf16[40,4096]{1,0:T(8,128)(2,1)S(1)} all-gather(bf16[40,2048]{1,0:T(8,128)(2,1)} %reshape.55), channel_id=1, replica_groups=mesh['dp'=4,'fsdp'=2,'expert'=4] {'fsdp'}, dimensions={1}, use_global_device_ids=true | all-gather | bytes 491520 | tf_op jit(solution)/shard_map/all_gather | solution.py:42
  33.0 0.0 all-to-all-done
  33.0 1.7 %reshape.53 = bf16[40,2048]{1,0:T(8,128)(2,1)} reshape(bf16[4,10,2048]{2,1,0:T(8,128)(2,1)} %all-to-all-done) | data formatting | bytes 327680 | tf_op jit(solution)/shard_map/reshape | solution.py:40
  34.6 0.0 copy-start.2
  34.7 6.8 %all_gather.12 = bf16[40,4096]{1,0:T(8,128)(2,1)S(1)} all-gather(bf16[40,2048]{1,0:T(8,128)(2,1)} %reshape.53), channel_id=1, replica_groups=mesh['dp'=4,'fsdp'=2,'expert'=4] {'fsdp'}, dimensions={1}, use_global_device_ids=true | all-gather | bytes 491520 | tf_op jit(solution)/shard_map/all_gather | solution.py:43
  41.4 0.0 copy-start.3
  41.4 2.6 %fusion.3 = f32[40,384]{1,0:T(8,128)S(1)} fusion(bf16[40,4096]{1,0:T(8,128)(2,1)S(1)} %all_gather.13, bf16[1,4096,384]{2,1,0:T(8,128)(2,1)} %param.11), kind=kOutput, calls=%fused_computation.4 | convolution fusion | flops 125829120 | bytes 3534848 | tf_op jit(solution)/shard_map/dot_general | solution.py:49
  44.0 0.0 copy-done.2
  44.0 0.0 copy-start.1
  44.0 1.0 fusion.8
  45.1 0.0 copy-done.3
  45.1 0.0 copy-done
  45.1 1.2 multiply_convert_fusion.2
  46.2 0.0 copy-done.1
  46.2 1.3 %fusion.1 = f32[40,4096]{1,0:T(8,128)S(1)} fusion(bf16[40,384]{1,0:T(8,128)(2,1)S(1)} %get-tuple-element.9, bf16[1,4096,384]{2,1,0:T(8,128)(2,1)S(1)} %copy-done.1), kind=kOutput, calls=%fused_computation.2 | convolution fusion | flops 125829120 | bytes 3831808 | tf_op jit(solution)/shard_map/dot_general | solution.py:59
  47.6 2.1 %fusion = bf16[40,4096]{1,0:T(8,128)(2,1)} fusion(f32[40,4096]{1,0:T(8,128)S(1)} %fusion.1, bf16[40,384]{1,0:T(8,128)(2,1)S(1)} %get-tuple-element.10, bf16[1,4096,384]{2,1,0:T(8,128)(2,1)S(1)} %copy-done), kind=kOutput, calls=%fused_computation.1 | convolution fusion | flops 126156800 | bytes 4159488 | tf_op jit(solution)/shard_map/dot_general | solution.py:60
  49.6 0.0 reduce-scatter.2.cloned.1.call-update
  49.7 13.5 %reduce-scatter.2.cloned.1.call-done = bf16[40,2048]{1,0:T(8,128)(2,1)} async-done(((bf16[40,4096]{1,0:T(8,128)(2,1)}), bf16[40,2048]{1,0:T(8,128)(2,1)}) %reduce-scatter.2.cloned.1.call-update) | async-done | bytes 163856 | tf_op jit(solution)/shard_map/reduce_scatter | solution.py:63
  63.2 1.7 %reshape.56 = bf16[4,10,2048]{2,1,0:T(8,128)(2,1)} reshape(bf16[40,2048]{1,0:T(8,128)(2,1)} %reduce-scatter.2.cloned.1.call-done) | data formatting | bytes 327680 | tf_op jit(solution)/shard_map/reshape | solution.py:67
  64.8 4.0 %all-to-all-start.2 = ((bf16[4,10,2048]{2,1,0:T(8,128)(2,1)}), bf16[4,10,2048]{2,1,0:T(8,128)(2,1)}, u32[]{:S(2)}, u32[]{:S(2)}) async-start(bf16[4,10,2048]{2,1,0:T(8,128)(2,1)} %reshape.56), calls=%async_computation.3 | async-start | bytes 524288 | tf_op jit(solution)/shard_map/all_to_all | solution.py:66
  68.9 1.0 pad_maximum_fusion
  69.9 0.9 copy.17
  70.8 4.2 %all-to-all-done.2 = bf16[4,10,2048]{2,1,0:T(8,128)(2,1)} async-done(((bf16[4,10,2048]{2,1,0:T(8,128)(2,1)}), bf16[4,10,2048]{2,1,0:T(8,128)(2,1)}, u32[]{:S(2)}, u32[]{:S(2)}) %all-to-all-start.2) | async-done | bytes 163872 | tf_op jit(solution)/shard_map/all_to_all | solution.py:66
  75.0 5.1 %all-to-all-start.3 = ((bf16[80,4,1024]{2,0,1:T(8,128)(2,1)}), bf16[80,4,1024]{2,0,1:T(8,128)(2,1)}, u32[]{:S(2)}, u32[]{:S(2)}) async-start(bf16[80,4,1024]{2,0,1:T(8,128)(2,1)} %bitcast.34), calls=%async_computation.4 | async-start | bytes 1310720 | tf_op jit(solution)/shard_map/all_to_all | solution.py:81
  80.1 0.8 pad_maximum_fusion.1
  80.9 24.2 %all-gather = bf16[40,4608]{1,0:T(8,128)(2,1)S(1)} all-gather(bf16[40,1152]{1,0:T(8,128)(2,1)S(1)} %pad_maximum_fusion.1), channel_id=2, replica_groups=mesh['dp'=4,'fsdp'=2,'expert'=4] {'dp'}, dimensions={1}, use_global_device_ids=true | all-gather | bytes 460800 | tf_op jit(solution)/shard_map/all_gather | solution.py:83
  105.1 1.0 reshape.59
  106.0 0.0 copy-start.4
  106.0 1.7 %reshape.57 = bf16[40,2048]{1,0:T(8,128)(2,1)} reshape(bf16[4,10,2048]{2,1,0:T(8,128)(2,1)} %all-to-all-done.2) | data formatting | bytes 327680 | tf_op jit(solution)/shard_map/reshape | solution.py:71
  107.8 2.1 %convolution_convert_fusion = bf16[128,2048]{1,0:T(8,128)(2,1)} fusion(bf16[40,2048]{1,0:T(8,128)(2,1)} %reshape.57, s32[128]{0:T(128)S(1)} %multiply_add_fusion), kind=kOutput, calls=%fused_computation.11 | convolution fusion | flops 21238784 | bytes 688640 | tf_op jit(solution)/shard_map/dot_general | solution.py:69
  109.8 0.0 all-to-all-done.3
  109.8 1.8 %fusion.20 = (bf16[40,4,1024]{2,0,1:T(8,128)(2,1)S(1)}, bf16[40,4,1024]{2,0,1:T(8,128)(2,1)}) fusion(bf16[80,4,1024]{2,0,1:T(8,128)(2,1)} %all-to-all-done.3), kind=kLoop, calls=%fused_computation.44 | loop fusion | bytes 1310720 | tf_op jit(solution)/shard_map/slice | solution.py:88
  111.7 1.0 copy.14
  112.6 1.8 %reshape_squeeze.7 = bf16[160,1024]{1,0:T(8,128)(2,1)} reshape(bf16[40,4,1024]{2,1,0:T(4,128)(2,1)} %copy.14) | data formatting | bytes 655360 | tf_op jit(solution)/shard_map/reshape;squeeze | solution.py:88
  114.4 2.0 %copy.13 = bf16[40,4,1024]{2,1,0:T(4,128)(2,1)} copy(bf16[40,4,1024]{2,0,1:T(8,128)(2,1)} %get-tuple-element.7) | data formatting | bytes 655360 | tf_op jit(solution)/shard_map/slice | solution.py:87
  116.4 1.8 %reshape_squeeze.6 = bf16[160,1024]{1,0:T(8,128)(2,1)} reshape(bf16[40,4,1024]{2,1,0:T(4,128)(2,1)} %copy.13) | data formatting | bytes 655360 | tf_op jit(solution)/shard_map/reshape;squeeze | solution.py:87
  118.1 0.0 copy-done.4
  118.1 2.2 %fusion.10 = bf16[1,384,1024]{2,1,0:T(8,128)(2,1)} fusion(bf16[160,1024]{1,0:T(8,128)(2,1)} %reshape_squeeze.7, bf16[160,1152]{1,0:T(8,128)(2,1)S(1)} %copy-done.4), kind=kOutput, calls=%fused_computation.16 | convolution fusion | flops 126222336 | bytes 1236992 | tf_op jit(solution)/shard_map/dot_general | solution.py:95
  120.4 1.6 %convolution_convert_fusion.3 = bf16[1024,768]{1,0:T(8,128)(2,1)S(1)} fusion(bf16[160,1024]{1,0:T(8,128)(2,1)} %reshape_squeeze.6, bf16[160,1152]{1,0:T(8,128)(2,1)S(1)} %copy-done.4), kind=kOutput, calls=%fused_computation.14 | convolution fusion | flops 252444672 | bytes 2146304 | tf_op jit(solution)/shard_map/dot_general | solution.py:90
  122.0 1.3 slice_bitcast_fusion
  (2 shorter events, 0.0 us)
Async XLA Ops:
  7.2 37.9 %copy-start = (bf16[1,4096,384]{2,1,0:T(8,128)(2,1)S(1)}, bf16[1,4096,384]{2,1,0:T(8,128)(2,1)}, u32[]{:S(2)}) copy-start(bf16[1,4096,384]{2,1,0:T(8,128)(2,1)} %param.12) | copy-start | bytes 9437188
  11.3 9.4 %all-to-all-start.1 = ((bf16[4,10,2048]{2,1,0:T(8,128)(2,1)}), bf16[4,10,2048]{2,1,0:T(8,128)(2,1)S(1)}, u32[]{:S(2)}, u32[]{:S(2)}) async-start(bf16[4,10,2048]{2,1,0:T(8,128)(2,1)} %reshape.54), calls=%async_computation.1 | async-start | bytes 524288 | tf_op jit(solution)/shard_map/all_to_all | solution.py:36
  20.7 12.2 %all-to-all-start = ((bf16[4,10,2048]{2,1,0:T(8,128)(2,1)}), bf16[4,10,2048]{2,1,0:T(8,128)(2,1)}, u32[]{:S(2)}, u32[]{:S(2)}) async-start(bf16[4,10,2048]{2,1,0:T(8,128)(2,1)} %reshape.52), calls=%async_computation | async-start | bytes 524288 | tf_op jit(solution)/shard_map/all_to_all | solution.py:37
  24.8 38.4 %reduce-scatter.2.cloned.1.call-start = ((), (), s32[]{:S(2)}) async-start(), calls=%async_computation.5 | async-start | bytes 491520 | tf_op jit(solution)/shard_map/reduce_scatter | solution.py:63
  34.6 9.3 %copy-start.2 = (bf16[1,384,4096]{2,1,0:T(8,128)(2,1)S(1)}, bf16[1,384,4096]{2,1,0:T(8,128)(2,1)}, u32[]{:S(2)}) copy-start(bf16[1,384,4096]{2,1,0:T(8,128)(2,1)} %param.13) | copy-start | bytes 9437188
  41.4 3.6 %copy-start.3 = (bf16[40,4096]{1,0:T(8,128)(2,1)}, bf16[40,4096]{1,0:T(8,128)(2,1)S(1)}, u32[]{:S(2)}) copy-start(bf16[40,4096]{1,0:T(8,128)(2,1)S(1)} %all_gather.12) | copy-start | bytes 983044
  44.0 2.3 %copy-start.1 = (bf16[1,4096,384]{2,1,0:T(8,128)(2,1)S(1)}, bf16[1,4096,384]{2,1,0:T(8,128)(2,1)}, u32[]{:S(2)}) copy-start(bf16[1,4096,384]{2,1,0:T(8,128)(2,1)} %param.11) | copy-start | bytes 9437188
  64.8 10.2 %all-to-all-start.2 = ((bf16[4,10,2048]{2,1,0:T(8,128)(2,1)}), bf16[4,10,2048]{2,1,0:T(8,128)(2,1)}, u32[]{:S(2)}, u32[]{:S(2)}) async-start(bf16[4,10,2048]{2,1,0:T(8,128)(2,1)} %reshape.56), calls=%async_computation.3 | async-start | bytes 524288 | tf_op jit(solution)/shard_map/all_to_all | solution.py:66
  75.0 34.8 %all-to-all-start.3 = ((bf16[80,4,1024]{2,0,1:T(8,128)(2,1)}), bf16[80,4,1024]{2,0,1:T(8,128)(2,1)}, u32[]{:S(2)}, u32[]{:S(2)}) async-start(bf16[80,4,1024]{2,0,1:T(8,128)(2,1)} %bitcast.34), calls=%async_computation.4 | async-start | bytes 1310720 | tf_op jit(solution)/shard_map/all_to_all | solution.py:81
  106.0 12.1 %copy-start.4 = (bf16[160,1152]{1,0:T(8,128)(2,1)S(1)}, bf16[160,1152]{1,0:T(8,128)(2,1)}, u32[]{:S(2)}) copy-start(bf16[160,1152]{1,0:T(8,128)(2,1)} %reshape.59) | copy-start | bytes 1105924
Sparse Core Ops, SparseCore 0:
  49.8 13.3 reduce-scatter.1

commit v2 on v0

v2 whole, which is shorter than its diff:
```python
import functools

import jax
import jax.numpy as jnp
import numpy as np
from jax import lax
from jax.experimental import pallas as pl
from jax.experimental.pallas import tpu as pltpu
from jax.sharding import PartitionSpec as P

CAP = 10
OUT_FOLD = 4
BACK_FOLD = 8
ROWS = 2 * CAP * OUT_FOLD
STRIDE = 4096.0
MESH = pl.DeviceIdType.MESH
F32 = jnp.float32
BF16 = jnp.bfloat16


def dot(a, b, ca=1, cb=0):
    return lax.dot_general(a, b, (((ca,), (cb,)), ((), ())), preferred_element_type=F32)


def kernel(
    groups, halves, owners,
    tokens, cotangent, routes, route_gates, gate_hbm, up_hbm, down_hbm, out_key, back_key, unpack, permute,
    token_grads, gate_grads, up_grads, down_grads,
    gate_w, up_w, down_w, packed, landed, rows_all, slices, mine, factors, back, returned,
    w_sem, send1, recv1, send2, recv2, send3, recv3, send4, recv4,
):
    g, f, e = lax.axis_index("dp"), lax.axis_index("fsdp"), lax.axis_index("expert")
    slots = owners * CAP
    quarter = tokens.shape[1]
    width = quarter // OUT_FOLD
    back_width = quarter // BACK_FOLD
    ff = gate_w.shape[1]
    part = slices.shape[2]
    plane = [(a, b) for a in range(halves) for b in range(owners) if (a, b) != (0, 0)]
    far = lambda a, b: (lax.rem(f + a, halves), lax.rem(e + b, owners))

    loads = [
        pltpu.make_async_copy(src.at[0], dst, w_sem.at[i])
        for i, (src, dst) in enumerate(((gate_hbm, gate_w), (up_hbm, up_w), (down_hbm, down_w)))
    ]
    for load in loads:
        load.start()

    barrier = pltpu.get_barrier_semaphore()
    for a, b in plane:
        pf, pe = far(a, b)
        pl.semaphore_signal(barrier, inc=1, device_id=(g, pf, pe), device_id_type=MESH)
    for k in range(1, groups):
        pl.semaphore_signal(
            barrier, inc=1, device_id=(lax.rem(g + k, groups), f, e), device_id_type=MESH
        )

    count = tokens.shape[0]
    ids = routes[...].astype(F32)
    inside = ids < float(owners)
    target = jnp.sum(jnp.where(inside, ids, 0.0), axis=1, keepdims=True)
    named = jnp.sum(jnp.where(inside, 1.0, 0.0), axis=1, keepdims=True)
    target = jnp.where(named > 0.0, target, float(owners))
    route_gate = jnp.sum(jnp.where(inside, route_gates[...], 0.0), axis=1, keepdims=True)
    scaled = (route_gate * cotangent[...].astype(F32)).astype(BF16)
    lanes = lax.broadcasted_iota(jnp.int32, (count, count), 1)
    subs = lax.broadcasted_iota(jnp.int32, (count, count), 0)
    onehot = jnp.where(lanes.astype(F32) == target, 1.0, 0.0)
    earlier = jnp.where(lanes < subs, 1.0, 0.0).astype(BF16)
    before = dot(earlier, onehot.astype(BF16))
    position = target * float(CAP) + jnp.sum(before * onehot, axis=1, keepdims=True)
    across = jnp.sum(jnp.where(lanes == subs, position, 0.0), axis=0, keepdims=True)

    key = out_key[...]
    picks, stacked = [], []
    for chunk in range(OUT_FOLD):
        for which, source in enumerate((tokens[...], scaled)):
            offset = STRIDE * (2 * chunk + which)
            picks.append(jnp.where(key == across + offset, 1.0, 0.0).astype(BF16))
            stacked.append(source[:, chunk * width : (chunk + 1) * width])
    sent = dot(jnp.concatenate(picks, axis=1), jnp.concatenate(stacked, axis=0))
    packed[...] = sent.astype(BF16).reshape(packed.shape)

    pl.semaphore_wait(barrier, len(plane) + groups - 1)
    outs = []
    for i, (a, b) in enumerate(plane):
        pf, pe = far(a, b)
        copy = pltpu.make_async_remote_copy(
            packed.at[pe], landed.at[f * owners + e], send1.at[i], recv1.at[f * owners + e],
            device_id=(g, pf, pe), device_id_type=MESH,
        )
        copy.start()
        outs.append(copy)
    landed[f * owners + e] = packed[e]

    for i, (a, b) in enumerate(plane):
        pf, pe = far(a, b)
        pltpu.make_async_remote_copy(
            packed.at[pe], landed.at[pf * owners + pe], send1.at[i], recv1.at[pf * owners + pe],
            device_id=(g, pf, pe), device_id_type=MESH,
        ).wait_recv()
    for half in range(halves):
        block = landed[half * owners : (half + 1) * owners].reshape(owners * ROWS, width)
        for chunk in range(OUT_FOLD):
            low = half * quarter + chunk * width
            rows_all[:, low : low + width] = dot(unpack[chunk], block).astype(BF16)
    for k in range(1, groups):
        d = lax.rem(g + k, groups)
        copy = pltpu.make_async_remote_copy(
            rows_all.at[:, pl.ds(pl.multiple_of(d * part, part), part)], slices.at[g],
            send2.at[k - 1], recv2.at[g], device_id=(d, f, e), device_id_type=MESH,
        )
        copy.start()
        outs.append(copy)
    slices[g] = rows_all[:, pl.ds(pl.multiple_of(g * part, part), part)]

    for load in loads:
        load.wait()
    full = rows_all[...]
    gate_pre = dot(full, gate_w[...])[:slots]
    up_pre = dot(full, up_w[...])[:slots]
    hidden_grad = dot(full, down_w[...], 1, 1)[slots:]
    sigmoid_gate = jax.nn.sigmoid(gate_pre)
    activated = gate_pre * sigmoid_gate
    hidden = activated * up_pre
    gate_grad = hidden_grad * up_pre * sigmoid_gate * (1.0 + gate_pre * (1.0 - sigmoid_gate))
    up_grad = hidden_grad * activated
    mine[...] = jnp.concatenate(
        [
            jnp.concatenate([gate_grad, up_grad], axis=1),
            jnp.concatenate([hidden, jnp.zeros_like(hidden)], axis=1),
        ],
        axis=0,
    ).astype(BF16)
    for k in range(1, groups):
        d = lax.rem(g + k, groups)
        copy = pltpu.make_async_remote_copy(
            mine, factors.at[g], send3.at[k - 1], recv3.at[g],
            device_id=(d, f, e), device_id_type=MESH,
        )
        copy.start()
        outs.append(copy)
    factors[g] = mine[...]

    gate_grad, up_grad = gate_grad.astype(BF16), up_grad.astype(BF16)
    for half in range(halves):
        terms = []
        for chunk in range(BACK_FOLD):
            low = half * quarter + chunk * back_width
            term = dot(gate_grad, gate_w[low : low + back_width, :], 1, 1)
            terms.append(term + dot(up_grad, up_w[low : low + back_width, :], 1, 1))
        ordered = dot(permute[...], jnp.concatenate(terms, axis=0).astype(BF16))
        back[half * owners : (half + 1) * owners] = ordered.astype(BF16).reshape(
            owners, ROWS, back_width
        )
    for i, (a, b) in enumerate(plane):
        pf, pe = far(a, b)
        copy = pltpu.make_async_remote_copy(
            back.at[pf * owners + pe], returned.at[f * owners + e], send4.at[i],
            recv4.at[f * owners + e], device_id=(g, pf, pe), device_id_type=MESH,
        )
        copy.start()
        outs.append(copy)
    returned[f * owners + e] = back[f * owners + e]

    for i, (a, b) in enumerate(plane):
        pf, pe = far(a, b)
        pltpu.make_async_remote_copy(
            back.at[pf * owners + pe], returned.at[pf * owners + pe], send4.at[i],
            recv4.at[pf * owners + pe], device_id=(g, pf, pe), device_id_type=MESH,
        ).wait_recv()
    come = returned[...].reshape(halves * owners * ROWS, back_width)
    place = jnp.broadcast_to(position, (count, back_key.shape[1]))
    for chunk in range(BACK_FOLD):
        pick = jnp.where(place + STRIDE * chunk == back_key[...], 1.0, 0.0).astype(BF16)
        low = chunk * back_width
        token_grads[:, low : low + back_width] = dot(pick, come).astype(BF16)

    for k in range(1, groups):
        d = lax.rem(g + k, groups)
        pltpu.make_async_remote_copy(
            rows_all.at[:, pl.ds(0, part)], slices.at[d], send2.at[k - 1], recv2.at[d],
            device_id=(d, f, e), device_id_type=MESH,
        ).wait_recv()
        pltpu.make_async_remote_copy(
            mine, factors.at[d], send3.at[k - 1], recv3.at[d],
            device_id=(d, f, e), device_id_type=MESH,
        ).wait_recv()
    many = groups * 2 * slots
    every = slices[...].reshape(many, part)
    top = lax.broadcasted_iota(jnp.int32, (groups, 2 * slots, ff), 1) < slots
    held = factors[...].astype(F32)
    low, high = held[:, :, :ff], held[:, :, ff:]
    for value, wanted, out in ((low, True, gate_grads), (high, True, up_grads)):
        value = jnp.where(top, value, 0.0).astype(BF16).reshape(many, ff)
        out[0] = dot(every, value, 0, 0).astype(BF16)
    value = jnp.where(top, 0.0, low).astype(BF16).reshape(many, ff)
    down_grads[0] = dot(value, every, 0, 0).astype(BF16)
    for copy in outs:
        copy.wait_send()


def local(groups, halves, owners, tokens, cotangent, routes, route_gates, gate_weight, up_weight, down_weight):
    quarter = tokens.shape[1]
    model, ff = gate_weight.shape[1:]
    slots = owners * CAP
    count = tokens.shape[0]
    part = model // groups
    width, back_width = quarter // OUT_FOLD, quarter // BACK_FOLD

    at = np.arange(owners * ROWS)
    owner, chunk = at // ROWS, at % ROWS // (2 * CAP)
    which, row = at % (2 * CAP) // CAP, at % CAP
    out_key = (owner * CAP + row + STRIDE * (2 * chunk + which)).astype(np.float32)
    out_key = np.broadcast_to(out_key[:, None], (owners * ROWS, count))
    spot = which * slots + owner * CAP + row
    unpack = np.stack([
        (spot[None, :] == np.arange(2 * slots)[:, None]) & (chunk == c)[None, :]
        for c in range(OUT_FOLD)
    ])
    back_chunk = at % ROWS // CAP
    slot = owner * CAP + row
    permute = (back_chunk * slots + slot)[:, None] == np.arange(BACK_FOLD * slots)[None, :]
    back_key = np.tile((slot + STRIDE * back_chunk).astype(np.float32), halves)[None, :]

    vmem = pl.BlockSpec(memory_space=pltpu.VMEM)
    anywhere = pl.BlockSpec(memory_space=pl.ANY)
    peers = halves * owners
    dma = pltpu.SemaphoreType.DMA
    return pl.pallas_call(
        functools.partial(kernel, groups, halves, owners),
        out_shape=(
            jax.ShapeDtypeStruct((count, quarter), BF16),
            jax.ShapeDtypeStruct((1, part, ff), BF16),
            jax.ShapeDtypeStruct((1, part, ff), BF16),
            jax.ShapeDtypeStruct((1, ff, part), BF16),
        ),
        in_specs=[vmem] * 4 + [anywhere] * 3 + [vmem] * 4,
        out_specs=(vmem,) * 4,
        scratch_shapes=[
            pltpu.VMEM((model, ff), BF16),
            pltpu.VMEM((model, ff), BF16),
            pltpu.VMEM((ff, model), BF16),
            pltpu.VMEM((owners, ROWS, width), BF16),
            pltpu.VMEM((peers, ROWS, width), BF16),
            pltpu.VMEM((2 * slots, model), BF16),
            pltpu.VMEM((groups, 2 * slots, part), BF16),
            pltpu.VMEM((2 * slots, 2 * ff), BF16),
            pltpu.VMEM((groups, 2 * slots, 2 * ff), BF16),
            pltpu.VMEM((peers, ROWS, back_width), BF16),
            pltpu.VMEM((peers, ROWS, back_width), BF16),
            dma((3,)),
            dma((peers,)),
            dma((peers,)),
            dma((groups,)),
            dma((groups,)),
            dma((groups,)),
            dma((groups,)),
            dma((peers,)),
            dma((peers,)),
        ],
        compiler_params=pltpu.CompilerParams(
            collective_id=0, has_side_effects=True, vmem_limit_bytes=56 * 1024 * 1024
        ),
    )(
        tokens, cotangent, routes, route_gates, gate_weight, up_weight, down_weight,
        jnp.asarray(out_key), jnp.asarray(back_key), jnp.asarray(unpack, BF16), jnp.asarray(permute, BF16),
    )


def solution(mesh):
    placed = (
        P(("dp", "expert"), "fsdp"),
        P(("dp", "expert"), "fsdp"),
        P(("dp", "expert"), None),
        P(("dp", "expert"), None),
        P("expert", None, "fsdp"),
        P("expert", None, "fsdp"),
        P("expert", "fsdp", None),
    )
    sizes = (mesh.shape["dp"], mesh.shape["fsdp"], mesh.shape["expert"])
    return jax.shard_map(
        functools.partial(local, *sizes),
        mesh=mesh,
        in_specs=placed,
        out_specs=(
            P(("dp", "expert"), "fsdp"),
            P("expert", "dp", "fsdp"),
            P("expert", "dp", "fsdp"),
            P("expert", "fsdp", "dp"),
        ),
        check_vma=False,
    )
```

time: 251 us -> 55.5 us (0.22)
  waiting for transfers between devices: 159 us -> 0 us
  Pallas kernels: 0 us -> 44.1 us
  blocking collectives: 23.4 us -> 0 us
  matrix products: 19.4 us -> 0 us
  between operations: 14.1 us -> 0.66 us
  other arithmetic: 10.6 us -> 0 us
  starting transfers between devices: 7.53 us -> 0 us
  local copies, waits for them, and re-layouts: 14.5 us -> 10.1 us
    reduce_scatter x2 -> x0, waiting for transfers between devices: 157 us -> none  [the longest x1 151 us: local(): lax.psum_scatter(jnp.concatenate([lax.dot_general(full_rows, gate_grad, c...]
    pallas_call x0 -> x1, Pallas kernels: none -> 44.1 us  [local(): pl.pallas_call(functools.partial(kernel, groups, halves, owners), out_sha...]
    dot_general x11 -> x0, matrix products: 19.4 us -> none  [the longest x1 3.49 us: local(): lax.dot_general(full_grads, hidden, contract, preferred_element_type=jnp....]
    all_gather x2 -> x0, blocking collectives: 14.3 us -> none  [the longest x1 7.55 us: local(): lax.all_gather(flat_rows, 'fsdp', axis=1, tiled=True)]
    all_to_all x1 -> x0, blocking collectives: 9.08 us -> none  [local(): lax.all_to_all(route_rows.reshape(owners, CAP, quarter), 'expert', split_...]
    concatenate x1 -> x0, other arithmetic: 7.75 us -> none  [local(): jnp.concatenate([lax.dot_general(full_rows, gate_grad, contract, preferre...]
    all_to_all x2 -> x0, starting transfers between devices: 7.45 us -> none  [the longest x1 4.04 us: local(): lax.all_to_all(send_grads, 'expert', split_axis=0, concat_axis=0, tiled=T...]
    reshape x6 -> x0, local copies, waits for them, and re-layouts: 6.83 us -> none  [the longest x1 1.68 us: local(): flat_grads = recv_grads.reshape(slot_count, quarter)]
  transfers between devices with their start and end apart: 4 -> 0, of which waited for: 3 -> 0; matrix products, arithmetic and copies ran while one was open for 7% -> 0% of each run, Pallas kernels for 0% -> 0%
where the time goes in v2:
time: 55.5 us; the launch traced here: 54.9 us
  Pallas kernels  44.1 us (79%)
  local copies, waits for them, and re-layouts  10.1 us (18%)
  between operations  0.66 us (1%)
    pallas_call x1, Pallas kernels, local(): pl.pallas_call(functools.partial(kernel, groups, halves, owners), out_sha...  44.1 us
    unnamed x10, local copies, waits for them, and re-layouts  8.69 us
    another operation x1, local copies, waits for them, and re-layouts  1.45 us

profile of v2, /device:TPU:8, one launch (start us, length us, event | category | flops | bytes accessed | tf_op | source)
XLA Modules:
  0.0 54.9 jit_solution(13898042917566598816)
XLA Ops:
  0.6 1.4 %copy.15.routes = s32[128,8]{1,0:T(8,128)} copy(s32[128,8]{0,1:T(8,128)} %param.13) | data formatting | bytes 8192 | tf_op args[2]
  2.0 1.4 %copy.16.route_gates = f32[128,8]{1,0:T(8,128)} copy(f32[128,8]{0,1:T(8,128)} %param.14) | data formatting | bytes 8192 | tf_op args[3]
  3.5 1.5 %jit_solution_.3.out_key = f32[320,128]{1,0:T(8,128)} broadcast(f32[320]{0:T(512)} %constant.8.clone), dimensions={0} | broadcast | bytes 165120 | tf_op jit(solution)
  4.9 44.1 %shard_map.138 = (bf16[128,2048]{1,0:T(8,128)(2,1)}, bf16[1,1024,384]{2,1,0:T(8,128)(2,1)}, bf16[1,1024,384]{2,1,0:T(8,128)(2,1)}, bf16[1,384,1024]{2,1,0:T(8,128)(2,1)}) custom-call(bf16[128,2048]{1,0:T(8,128)(2,1)} %tokens.1, bf16[128,2048]{1,0:T(8,128)(2,1)} %cotangent.1, s32[128,8]{1,0:T(8,128)} %copy.15.routes, f32[128,8]{1,0:T(8,128)} %copy.16.route_gates, ...), custom_call_target="tpu_custom_call" | custom-call | tf_op jit(solution)/shard_map/pallas_call | solution.py:230
  49.1 0.0 copy-start.1
  49.1 0.0 copy-start
  49.1 2.0 %copy.21 = bf16[128,2048]{1,0:T(8,128)(2,1)} copy(bf16[128,2048]{1,0:T(8,128)(2,1)} %get-tuple-element.8) | data formatting | bytes 1048576
  51.1 2.1 %copy.22 = bf16[1,1024,384]{2,1,0:T(8,128)(2,1)} copy(bf16[1,1024,384]{2,1,0:T(8,128)(2,1)} %get-tuple-element.9) | data formatting | bytes 1572864
  53.2 0.0 copy-done.1
  53.2 0.9 %copy.23 = bf16[1,1024,384]{2,1,0:T(8,128)(2,1)} copy(bf16[1,1024,384]{2,1,0:T(8,128)(2,1)S(1)} %copy-done.1) | data formatting | bytes 1572864
  54.0 0.0 copy-done
  54.0 0.9 %copy.24 = bf16[1,384,1024]{2,1,0:T(8,128)(2,1)} copy(bf16[1,384,1024]{2,1,0:T(8,128)(2,1)S(1)} %copy-done) | data formatting | bytes 1572864
Async XLA Ops:
  49.1 4.1 %copy-start.1 = (bf16[1,1024,384]{2,1,0:T(8,128)(2,1)S(1)}, bf16[1,1024,384]{2,1,0:T(8,128)(2,1)}, u32[]{:S(2)}) copy-start(bf16[1,1024,384]{2,1,0:T(8,128)(2,1)} %get-tuple-element.10) | copy-start | bytes 2359300
  49.1 5.0 %copy-start = (bf16[1,384,1024]{2,1,0:T(8,128)(2,1)S(1)}, bf16[1,384,1024]{2,1,0:T(8,128)(2,1)}, u32[]{:S(2)}) copy-start(bf16[1,384,1024]{2,1,0:T(8,128)(2,1)} %get-tuple-element.11) | copy-start | bytes 2359300

commit v3 on v2

v3 whole, which is shorter than its diff:
```python
import functools

import jax
import jax.numpy as jnp
import numpy as np
from jax import lax
from jax.experimental import pallas as pl
from jax.experimental.pallas import tpu as pltpu
from jax.sharding import PartitionSpec as P

CAP = 10
OUT_FOLD = 4
BACK_FOLD = 8
ROWS = 2 * CAP * OUT_FOLD
STRIDE = 4096.0
MESH = pl.DeviceIdType.MESH
F32 = jnp.float32
BF16 = jnp.bfloat16


def dot(a, b, ca=1, cb=0):
    return lax.dot_general(a, b, (((ca,), (cb,)), ((), ())), preferred_element_type=F32)


def place(routes, owners):
    ids = routes.astype(F32)
    inside = ids < float(owners)
    target = jnp.sum(jnp.where(inside, ids, 0.0), axis=0, keepdims=True)
    named = jnp.sum(jnp.where(inside, 1.0, 0.0), axis=0, keepdims=True)
    target = jnp.where(named > 0.0, target, float(owners))
    count = routes.shape[1]
    lanes = lax.broadcasted_iota(jnp.int32, (count, count), 1)
    subs = lax.broadcasted_iota(jnp.int32, (count, count), 0)
    onehot = jnp.where(subs.astype(F32) == target, 1.0, 0.0)
    earlier = jnp.where(subs < lanes, 1.0, 0.0).astype(BF16)
    before = dot(onehot.astype(BF16), earlier)
    position = target * float(CAP) + jnp.sum(before * onehot, axis=0, keepdims=True)
    return inside, position, lanes == subs


def column(row, diagonal):
    return jnp.sum(jnp.where(diagonal, row, 0.0), axis=1, keepdims=True)


def folded(shape, axis):
    at = lax.broadcasted_iota(jnp.int32, shape, axis).astype(F32)
    owner = jnp.floor((at + 0.5) * (1.0 / ROWS))
    at = at - owner * ROWS
    fold = jnp.floor((at + 0.5) * (1.0 / CAP))
    return owner * CAP + (at - fold * CAP), fold


def kernel(
    groups, halves, owners,
    tokens, cotangent, routes, route_gates, gate_hbm, up_hbm, down_hbm,
    slices, factors, returned,
    gate_w, up_w, down_w, packed, landed, rows_all, mine, back,
    w_sem, send1, recv1, send2, recv2, send3, recv3, send4, recv4, send5, recv5,
):
    g, f, e = lax.axis_index("dp"), lax.axis_index("fsdp"), lax.axis_index("expert")
    slots = owners * CAP
    quarter = tokens.shape[1]
    width = quarter // OUT_FOLD
    back_width = quarter // BACK_FOLD
    part = slices.shape[2]
    plane = [(a, b) for a in range(halves) for b in range(owners) if (a, b) != (0, 0)]
    far = lambda a, b: (lax.rem(f + a, halves), lax.rem(e + b, owners))
    shared = halves > 1 and part % (128 * halves) == 0
    share = part // halves if shared else part

    def columns(start):
        return pl.ds(pl.multiple_of(start, share), share)

    def own_share(half):
        return columns(half * share if shared else 0)

    loads = [
        pltpu.make_async_copy(src.at[0], dst, w_sem.at[i])
        for i, (src, dst) in enumerate(((gate_hbm, gate_w), (up_hbm, up_w), (down_hbm, down_w)))
    ]
    for load in loads:
        load.start()

    barrier = pltpu.get_barrier_semaphore()
    for a, b in plane:
        pf, pe = far(a, b)
        pl.semaphore_signal(barrier, inc=1, device_id=(g, pf, pe), device_id_type=MESH)
    for k in range(1, groups):
        pl.semaphore_signal(
            barrier, inc=1, device_id=(lax.rem(g + k, groups), f, e), device_id_type=MESH
        )

    inside, position, diagonal = place(routes[...], owners)
    route_gate = jnp.sum(jnp.where(inside, route_gates[...], 0.0), axis=0, keepdims=True)
    scaled = (column(route_gate, diagonal) * cotangent[...].astype(F32)).astype(BF16)

    slot, fold = folded((owners * ROWS, tokens.shape[0]), 0)
    key = slot + STRIDE * fold
    picks, stacked = [], []
    for chunk in range(OUT_FOLD):
        for which, source in enumerate((tokens[...], scaled)):
            offset = STRIDE * (2 * chunk + which)
            picks.append(jnp.where(key == position + offset, 1.0, 0.0).astype(BF16))
            stacked.append(source[:, chunk * width : (chunk + 1) * width])
    sent = dot(jnp.concatenate(picks, axis=1), jnp.concatenate(stacked, axis=0))
    packed[...] = sent.astype(BF16).reshape(packed.shape)

    pl.semaphore_wait(barrier, len(plane) + groups - 1)
    outs = []
    for i, (a, b) in reversed(list(enumerate(plane))):
        pf, pe = far(a, b)
        copy = pltpu.make_async_remote_copy(
            packed.at[pe], landed.at[f * owners + e], send1.at[i], recv1.at[f * owners + e],
            device_id=(g, pf, pe), device_id_type=MESH,
        )
        copy.start()
        outs.append(copy)
    landed[f * owners + e] = packed[e]

    slot, fold = folded((2 * slots, owners * ROWS), 1)
    chunk_of = jnp.floor(fold * 0.5 + 0.25)
    spot = slot + slots * (fold - 2.0 * chunk_of) + 2 * slots * chunk_of
    at = lax.broadcasted_iota(jnp.int32, spot.shape, 0).astype(F32)
    unpack = [
        jnp.where(spot == at + 2.0 * slots * c, 1.0, 0.0).astype(BF16) for c in range(OUT_FOLD)
    ]
    slot, fold = folded((owners * ROWS, BACK_FOLD * slots), 0)
    at = lax.broadcasted_iota(jnp.int32, slot.shape, 1).astype(F32)
    permute = jnp.where(fold * slots + slot == at, 1.0, 0.0).astype(BF16)

    gate_pre, up_pre, hidden_grad = 0.0, 0.0, 0.0
    for step in range(halves):
        half = lax.rem(f + step, halves)
        for i, (a, b) in enumerate(plane):
            if a == step:
                pf, pe = far(a, b)
                pltpu.make_async_remote_copy(
                    packed.at[pe], landed.at[pf * owners + pe], send1.at[i],
                    recv1.at[pf * owners + pe], device_id=(g, pf, pe), device_id_type=MESH,
                ).wait_recv()
        block = landed[pl.ds(half * owners, owners)].reshape(owners * ROWS, width)
        for chunk in range(OUT_FOLD):
            low = pl.multiple_of(half * quarter + chunk * width, width)
            rows_all[:, pl.ds(low, width)] = dot(unpack[chunk], block).astype(BF16)
        if step == halves - 1:
            for k in range(1, groups):
                d = lax.rem(g + k, groups)
                start = d * part + (f * share if shared else 0)
                copy = pltpu.make_async_remote_copy(
                    rows_all.at[:, columns(start)], slices.at[g, :, own_share(f)],
                    send2.at[k - 1], recv2.at[g], device_id=(d, f, e), device_id_type=MESH,
                )
                copy.start()
                outs.append(copy)
            slices[g] = rows_all[:, pl.ds(pl.multiple_of(g * part, part), part)]
        if step == 0:
            for load in loads:
                load.wait()
        span = pl.ds(pl.multiple_of(half * quarter, quarter), quarter)
        full = rows_all[:, span]
        gate_pre += dot(full, gate_w[span, :])
        up_pre += dot(full, up_w[span, :])
        hidden_grad += dot(full, down_w[:, span], 1, 1)

    gate_pre, up_pre, hidden_grad = gate_pre[:slots], up_pre[:slots], hidden_grad[slots:]
    sigmoid_gate = jax.nn.sigmoid(gate_pre)
    activated = gate_pre * sigmoid_gate
    hidden = activated * up_pre
    gate_grad = hidden_grad * up_pre * sigmoid_gate * (1.0 + gate_pre * (1.0 - sigmoid_gate))
    up_grad = hidden_grad * activated
    mine[...] = jnp.concatenate(
        [
            jnp.concatenate([gate_grad, up_grad], axis=1),
            jnp.concatenate([hidden, jnp.zeros_like(hidden)], axis=1),
        ],
        axis=0,
    ).astype(BF16)
    for k in range(1, groups):
        d = lax.rem(g + k, groups)
        copy = pltpu.make_async_remote_copy(
            mine, factors.at[g], send3.at[k - 1], recv3.at[g],
            device_id=(d, f, e), device_id_type=MESH,
        )
        copy.start()
        outs.append(copy)
    factors[g] = mine[...]

    gate_grad, up_grad = gate_grad.astype(BF16), up_grad.astype(BF16)
    for half in range(halves):
        terms = []
        for chunk in range(BACK_FOLD):
            low = half * quarter + chunk * back_width
            term = dot(gate_grad, gate_w[low : low + back_width, :], 1, 1)
            terms.append(term + dot(up_grad, up_w[low : low + back_width, :], 1, 1))
        ordered = dot(permute, jnp.concatenate(terms, axis=0).astype(BF16))
        back[half * owners : (half + 1) * owners] = ordered.astype(BF16).reshape(
            owners, ROWS, back_width
        )
    for i, (a, b) in enumerate(plane):
        pf, pe = far(a, b)
        copy = pltpu.make_async_remote_copy(
            back.at[pf * owners + pe], returned.at[f * owners + e], send4.at[i],
            recv4.at[f * owners + e], device_id=(g, pf, pe), device_id_type=MESH,
        )
        copy.start()
        outs.append(copy)
    returned[f * owners + e] = back[f * owners + e]

    for k in range(1, groups):
        d = lax.rem(g + k, groups)
        pltpu.make_async_remote_copy(
            rows_all.at[:, columns(0)], slices.at[d, :, own_share(f)], send2.at[k - 1],
            recv2.at[d], device_id=(d, f, e), device_id_type=MESH,
        ).wait_recv()
        if shared:
            for a in range(1, halves):
                pf = lax.rem(f + a, halves)
                copy = pltpu.make_async_remote_copy(
                    slices.at[d, :, own_share(f)], slices.at[d, :, own_share(f)],
                    send5.at[(k - 1) * halves + a], recv5.at[d * halves + f],
                    device_id=(g, pf, e), device_id_type=MESH,
                )
                copy.start()
                outs.append(copy)

    for i, (a, b) in enumerate(plane):
        pf, pe = far(a, b)
        pltpu.make_async_remote_copy(
            back.at[pf * owners + pe], returned.at[pf * owners + pe], send4.at[i],
            recv4.at[pf * owners + pe], device_id=(g, pf, pe), device_id_type=MESH,
        ).wait_recv()
    for k in range(1, groups):
        d = lax.rem(g + k, groups)
        pltpu.make_async_remote_copy(
            mine, factors.at[d], send3.at[k - 1], recv3.at[d],
            device_id=(d, f, e), device_id_type=MESH,
        ).wait_recv()
        if shared:
            for a in range(1, halves):
                pf = lax.rem(f + a, halves)
                pltpu.make_async_remote_copy(
                    slices.at[d, :, own_share(pf)], slices.at[d, :, own_share(pf)],
                    send5.at[(k - 1) * halves + a], recv5.at[d * halves + pf],
                    device_id=(g, pf, e), device_id_type=MESH,
                ).wait_recv()
    for copy in outs:
        copy.wait_send()


def finish(owners, routes, slices, factors, returned, back_key, token_grads, gate_grads, up_grads, down_grads):
    groups, rows, part = slices.shape
    ff = down_grads.shape[1]
    many = groups * rows
    every = slices[...].reshape(many, part)
    top = lax.broadcasted_iota(jnp.int32, factors.shape, 1) < rows // 2
    held = factors[...].astype(F32)
    value = jnp.where(top, held, 0.0).astype(BF16).reshape(many, 2 * ff)
    both = dot(every, value, 0, 0).astype(BF16)
    gate_grads[0] = both[:, :ff]
    up_grads[0] = both[:, ff:]
    value = jnp.where(top, 0.0, held)[:, :, :ff].astype(BF16).reshape(many, ff)
    down_grads[0] = dot(value, every, 0, 0).astype(BF16)

    peers, back_rows, back_width = returned.shape
    come = returned[...].reshape(peers * back_rows, back_width)
    _, position, diagonal = place(routes[...], owners)
    position = column(position, diagonal)
    position = jnp.broadcast_to(position, (position.shape[0], back_key.shape[1]))
    for chunk in range(BACK_FOLD):
        pick = jnp.where(position + STRIDE * chunk == back_key[...], 1.0, 0.0).astype(BF16)
        low = chunk * back_width
        token_grads[:, low : low + back_width] = dot(pick, come).astype(BF16)


def local(groups, halves, owners, tokens, cotangent, routes, route_gates, gate_weight, up_weight, down_weight):
    quarter = tokens.shape[1]
    model, ff = gate_weight.shape[1:]
    slots = owners * CAP
    count = tokens.shape[0]
    part = model // groups
    width, back_width = quarter // OUT_FOLD, quarter // BACK_FOLD
    at = np.arange(owners * ROWS)
    back_chunk, slot = at % ROWS // CAP, at // ROWS * CAP + at % CAP
    back_key = np.tile((slot + STRIDE * back_chunk).astype(np.float32), halves)[None, :]

    vmem = pl.BlockSpec(memory_space=pltpu.VMEM)
    anywhere = pl.BlockSpec(memory_space=pl.ANY)
    peers = halves * owners
    dma = pltpu.SemaphoreType.DMA
    turned = routes.T
    slices, factors, returned = pl.pallas_call(
        functools.partial(kernel, groups, halves, owners),
        out_shape=(
            jax.ShapeDtypeStruct((groups, 2 * slots, part), BF16),
            jax.ShapeDtypeStruct((groups, 2 * slots, 2 * ff), BF16),
            jax.ShapeDtypeStruct((peers, ROWS, back_width), BF16),
        ),
        in_specs=[vmem] * 4 + [anywhere] * 3,
        out_specs=(vmem,) * 3,
        scratch_shapes=[
            pltpu.VMEM((model, ff), BF16),
            pltpu.VMEM((model, ff), BF16),
            pltpu.VMEM((ff, model), BF16),
            pltpu.VMEM((owners, ROWS, width), BF16),
            pltpu.VMEM((peers, ROWS, width), BF16),
            pltpu.VMEM((2 * slots, model), BF16),
            pltpu.VMEM((2 * slots, 2 * ff), BF16),
            pltpu.VMEM((peers, ROWS, back_width), BF16),
            dma((3,)),
            dma((peers,)),
            dma((peers,)),
            dma((groups,)),
            dma((groups,)),
            dma((groups,)),
            dma((groups,)),
            dma((peers,)),
            dma((peers,)),
            dma((groups * halves,)),
            dma((groups * halves,)),
        ],
        compiler_params=pltpu.CompilerParams(
            collective_id=0, has_side_effects=True, vmem_limit_bytes=56 * 1024 * 1024
        ),
    )(
        tokens, cotangent, turned, route_gates.T, gate_weight, up_weight, down_weight,
    )
    return pl.pallas_call(
        functools.partial(finish, owners),
        out_shape=(
            jax.ShapeDtypeStruct((count, quarter), BF16),
            jax.ShapeDtypeStruct((1, part, ff), BF16),
            jax.ShapeDtypeStruct((1, part, ff), BF16),
            jax.ShapeDtypeStruct((1, ff, part), BF16),
        ),
        in_specs=[vmem] * 5,
        out_specs=(vmem,) * 4,
        compiler_params=pltpu.CompilerParams(vmem_limit_bytes=40 * 1024 * 1024),
    )(turned, slices, factors, returned, jnp.asarray(back_key))


def solution(mesh):
    placed = (
        P(("dp", "expert"), "fsdp"),
        P(("dp", "expert"), "fsdp"),
        P(("dp", "expert"), None),
        P(("dp", "expert"), None),
        P("expert", None, "fsdp"),
        P("expert", None, "fsdp"),
        P("expert", "fsdp", None),
    )
    sizes = (mesh.shape["dp"], mesh.shape["fsdp"], mesh.shape["expert"])
    return jax.shard_map(
        functools.partial(local, *sizes),
        mesh=mesh,
        in_specs=placed,
        out_specs=(
            P(("dp", "expert"), "fsdp"),
            P("expert", "dp", "fsdp"),
            P("expert", "dp", "fsdp"),
            P("expert", "fsdp", "dp"),
        ),
        check_vma=False,
    )
```

time: 55.5 us -> 42.9 us (0.77)
  local copies, waits for them, and re-layouts: 10.1 us -> 3.09 us
  Pallas kernels: 44.1 us -> 38.8 us
    pallas_call x1, Pallas kernels: 44.1 us -> 35.6 us  [local(): pl.pallas_call(functools.partial(kernel, groups, halves, owners), out_sha...]
    unnamed x10, local copies, waits for them, and re-layouts: 8.69 us -> 3.09 us
    pallas_call x0 -> x1, Pallas kernels: none -> 3.25 us  [local(): pl.pallas_call(functools.partial(finish, owners), out_shape=(jax.ShapeDty...]
    another operation x1 -> x0, local copies, waits for them, and re-layouts: 1.45 us -> none
where the time goes in v3:
time: 42.9 us; the launch traced here: 42.6 us
  Pallas kernels  38.8 us (90%)
  local copies, waits for them, and re-layouts  3.09 us (7%)
  between operations  0.68 us (2%)
    pallas_call x1, Pallas kernels, local(): pl.pallas_call(functools.partial(kernel, groups, halves, owners), out_sha...  35.6 us
    pallas_call x1, Pallas kernels, local(): pl.pallas_call(functools.partial(finish, owners), out_shape=(jax.ShapeDty...  3.25 us
    unnamed x10, local copies, waits for them, and re-layouts  3.09 us

profile of v3, /device:TPU:8, one launch (start us, length us, event | category | flops | bytes accessed | tf_op | source)
XLA Modules:
  0.0 42.6 jit_solution(3292459725374919307)
XLA Ops:
  0.6 0.0 copy-start.3
  0.6 0.0 copy-start.4
  0.7 35.6 %shard_map.111 = (bf16[4,80,1024]{2,1,0:T(8,128)(2,1)}, bf16[4,80,768]{2,1,0:T(8,128)(2,1)}, bf16[8,80,256]{2,1,0:T(8,128)(2,1)}) custom-call(bf16[128,2048]{1,0:T(8,128)(2,1)} %tokens.1, bf16[128,2048]{1,0:T(8,128)(2,1)} %cotangent.1, s32[8,128]{1,0:T(8,128)} %bitcast.2, f32[8,128]{1,0:T(8,128)} %bitcast.4, bf16[1,4096,384]{2,1,0:T(8,128)(2,1)} %gate_hbm.1, ...), custom_call_target="tpu_custom_call" | custom-call | tf_op jit(solution)/shard_map/pallas_call | solution.py:291
  36.2 0.0 copy-done.3
  36.3 0.0 copy-done.4
  36.3 0.0 copy-start
  36.3 1.1 %copy-done = bf16[4,80,1024]{2,1,0:T(8,128)(2,1)S(1)} copy-done((bf16[4,80,1024]{2,1,0:T(8,128)(2,1)S(1)}, bf16[4,80,1024]{2,1,0:T(8,128)(2,1)}, u32[]{:S(2)}) %copy-start) | copy-done | bytes 655384
  37.4 0.0 copy-start.1
  37.4 1.0 %copy-done.1 = bf16[4,80,768]{2,1,0:T(8,128)(2,1)S(1)} copy-done((bf16[4,80,768]{2,1,0:T(8,128)(2,1)S(1)}, bf16[4,80,768]{2,1,0:T(8,128)(2,1)}, u32[]{:S(2)}) %copy-start.1) | copy-done | bytes 491544
  38.4 0.0 copy-start.2
  38.4 1.0 %copy-done.2 = bf16[8,80,256]{2,1,0:T(8,128)(2,1)S(1)} copy-done((bf16[8,80,256]{2,1,0:T(8,128)(2,1)S(1)}, bf16[8,80,256]{2,1,0:T(8,128)(2,1)}, u32[]{:S(2)}) %copy-start.2) | copy-done | bytes 327704
  39.4 3.2 %shard_map.112 = (bf16[128,2048]{1,0:T(8,128)(2,1)}, bf16[1,1024,384]{2,1,0:T(8,128)(2,1)}, bf16[1,1024,384]{2,1,0:T(8,128)(2,1)}, bf16[1,384,1024]{2,1,0:T(8,128)(2,1)}) custom-call(s32[8,128]{1,0:T(8,128)S(1)} %bitcast.3, bf16[4,80,1024]{2,1,0:T(8,128)(2,1)S(1)} %copy-done, bf16[4,80,768]{2,1,0:T(8,128)(2,1)S(1)} %copy-done.1, ...), custom_call_target="tpu_custom_call" | custom-call | tf_op jit(solution)/shard_map/pallas_call | solution.py:327
Async XLA Ops:
  0.6 35.6 %copy-start.3 = (s32[128,8]{0,1:T(8,128)S(1)}, s32[128,8]{0,1:T(8,128)}, u32[]{:S(2)}) copy-start(s32[128,8]{0,1:T(8,128)} %param.10) | copy-start | bytes 12292
  0.6 35.6 %copy-start.4 = (f32[1,640]{1,0:T(1,128)S(1)}, f32[1,640]{1,0:T(1,128)}, u32[]{:S(2)}) copy-start(f32[1,640]{1,0:T(1,128)} %constant.2.clone.back_key) | copy-start | bytes 7684
  36.3 1.1 %copy-start = (bf16[4,80,1024]{2,1,0:T(8,128)(2,1)S(1)}, bf16[4,80,1024]{2,1,0:T(8,128)(2,1)}, u32[]{:S(2)}) copy-start(bf16[4,80,1024]{2,1,0:T(8,128)(2,1)} %get-tuple-element.7.slices) | copy-start | bytes 1966084
  37.4 1.0 %copy-start.1 = (bf16[4,80,768]{2,1,0:T(8,128)(2,1)S(1)}, bf16[4,80,768]{2,1,0:T(8,128)(2,1)}, u32[]{:S(2)}) copy-start(bf16[4,80,768]{2,1,0:T(8,128)(2,1)} %get-tuple-element.8.factors) | copy-start | bytes 1474564
  38.4 1.0 %copy-start.2 = (bf16[8,80,256]{2,1,0:T(8,128)(2,1)S(1)}, bf16[8,80,256]{2,1,0:T(8,128)(2,1)}, u32[]{:S(2)}) copy-start(bf16[8,80,256]{2,1,0:T(8,128)(2,1)} %get-tuple-element.9.returned) | copy-start | bytes 983044

commit v4 on v3

--- a/solution.py
+++ b/solution.py
@@ -247,29 +247,56 @@
         copy.wait_send()
 
 
-def finish(owners, routes, slices, factors, returned, back_key, token_grads, gate_grads, up_grads, down_grads):
+def finish(
+    owners, routes, slices_hbm, factors_hbm, returned_hbm, back_key, token_out, gate_out, up_out, down_out,
+    slices, factors, returned, token_grads, gate_grads, up_grads, down_grads, in_sem, out_sem,
+):
+    loads = [
+        pltpu.make_async_copy(src, dst, in_sem.at[i])
+        for i, (src, dst) in enumerate(
+            ((returned_hbm, returned), (slices_hbm, slices), (factors_hbm, factors))
+        )
+    ]
+    for load in loads:
+        load.start()
+    stores = [
+        pltpu.make_async_copy(src, dst, out_sem.at[i])
+        for i, (src, dst) in enumerate((
+            (token_grads, token_out), (gate_grads, gate_out.at[0]), (up_grads, up_out.at[0]),
+            (down_grads, down_out.at[0]),
+        ))
+    ]
+    _, position, diagonal = place(routes[...], owners)
+    position = column(position, diagonal)
+    position = jnp.broadcast_to(position, (position.shape[0], back_key.shape[1]))
+    peers, back_rows, back_width = returned.shape
+    loads[0].wait()
+    come = returned[...].reshape(peers * back_rows, back_width)
+    for chunk in range(BACK_FOLD):
+        pick = jnp.where(position + STRIDE * chunk == back_key[...], 1.0, 0.0).astype(BF16)
+        low = chunk * back_width
+        token_grads[:, low : low + back_width] = dot(pick, come).astype(BF16)
+    stores[0].start()
+
+    loads[1].wait()
+    loads[2].wait()
     groups, rows, part = slices.shape
-    ff = down_grads.shape[1]
+    ff = down_grads.shape[0]
     many = groups * rows
     every = slices[...].reshape(many, part)
     top = lax.broadcasted_iota(jnp.int32, factors.shape, 1) < rows // 2
     held = factors[...].astype(F32)
     value = jnp.where(top, held, 0.0).astype(BF16).reshape(many, 2 * ff)
     both = dot(every, value, 0, 0).astype(BF16)
-    gate_grads[0] = both[:, :ff]
-    up_grads[0] = both[:, ff:]
+    gate_grads[...] = both[:, :ff]
+    up_grads[...] = both[:, ff:]
+    stores[1].start()
+    stores[2].start()
     value = jnp.where(top, 0.0, held)[:, :, :ff].astype(BF16).reshape(many, ff)
-    down_grads[0] = dot(value, every, 0, 0).astype(BF16)
-
-    peers, back_rows, back_width = returned.shape
-    come = returned[...].reshape(peers * back_rows, back_width)
-    _, position, diagonal = place(routes[...], owners)
-    position = column(position, diagonal)
-    position = jnp.broadcast_to(position, (position.shape[0], back_key.shape[1]))
-    for chunk in range(BACK_FOLD):
-        pick = jnp.where(position + STRIDE * chunk == back_key[...], 1.0, 0.0).astype(BF16)
-        low = chunk * back_width
-        token_grads[:, low : low + back_width] = dot(pick, come).astype(BF16)
+    down_grads[...] = dot(value, every, 0, 0).astype(BF16)
+    stores[3].start()
+    for store in stores:
+        store.wait()
 
 
 def local(groups, halves, owners, tokens, cotangent, routes, route_gates, gate_weight, up_weight, down_weight):
@@ -332,9 +359,20 @@
             jax.ShapeDtypeStruct((1, part, ff), BF16),
             jax.ShapeDtypeStruct((1, ff, part), BF16),
         ),
-        in_specs=[vmem] * 5,
-        out_specs=(vmem,) * 4,
-        compiler_params=pltpu.CompilerParams(vmem_limit_bytes=40 * 1024 * 1024),
+        in_specs=[vmem] + [pl.BlockSpec(memory_space=pltpu.HBM)] * 3 + [vmem],
+        out_specs=(pl.BlockSpec(memory_space=pltpu.HBM),) * 4,
+        scratch_shapes=[
+            pltpu.VMEM((groups, 2 * slots, part), BF16),
+            pltpu.VMEM((groups, 2 * slots, 2 * ff), BF16),
+            pltpu.VMEM((peers, ROWS, back_width), BF16),
+            pltpu.VMEM((count, quarter), BF16),
+            pltpu.VMEM((part, ff), BF16),
+            pltpu.VMEM((part, ff), BF16),
+            pltpu.VMEM((ff, part), BF16),
+            dma((3,)),
+            dma((4,)),
+        ],
+        compiler_params=pltpu.CompilerParams(vmem_limit_bytes=56 * 1024 * 1024),
     )(turned, slices, factors, returned, jnp.asarray(back_key))
 
 

time: 42.9 us -> 41.2 us (0.960)
  local copies, waits for them, and re-layouts: 3.09 us -> 0 us
  Pallas kernels: 38.8 us -> 40.3 us
    unnamed x10 -> x0, local copies, waits for them, and re-layouts: 3.09 us -> none
    pallas_call x1, Pallas kernels: 3.25 us -> 4.69 us  [local(): pl.pallas_call(functools.partial(finish, owners), out_shape=(jax.ShapeDty...]
where the time goes in v4:
time: 41.2 us; the launch traced here: 40.9 us
  Pallas kernels  40.3 us (98%)
  between operations  0.64 us (2%)
    pallas_call x1, Pallas kernels, local(): pl.pallas_call(functools.partial(kernel, groups, halves, owners), out_sha...  35.6 us
    pallas_call x1, Pallas kernels, local(): pl.pallas_call(functools.partial(finish, owners), out_shape=(jax.ShapeDty...  4.69 us

profile of v4, /device:TPU:8, one launch (start us, length us, event | category | flops | bytes accessed | tf_op | source)
XLA Modules:
  0.0 40.9 jit_solution(17717804241472299795)
XLA Ops:
  0.6 35.6 %shard_map.111 = (bf16[4,80,1024]{2,1,0:T(8,128)(2,1)}, bf16[4,80,768]{2,1,0:T(8,128)(2,1)}, bf16[8,80,256]{2,1,0:T(8,128)(2,1)}) custom-call(bf16[128,2048]{1,0:T(8,128)(2,1)} %tokens.1, bf16[128,2048]{1,0:T(8,128)(2,1)} %cotangent.1, s32[8,128]{1,0:T(8,128)} %bitcast.2, f32[8,128]{1,0:T(8,128)} %bitcast.4, bf16[1,4096,384]{2,1,0:T(8,128)(2,1)} %gate_hbm.1, ...), custom_call_target="tpu_custom_call" | custom-call | tf_op jit(solution)/shard_map/pallas_call | solution.py:318
  36.3 4.7 %shard_map.112 = (bf16[128,2048]{1,0:T(8,128)(2,1)}, bf16[1,1024,384]{2,1,0:T(8,128)(2,1)}, bf16[1,1024,384]{2,1,0:T(8,128)(2,1)}, bf16[1,384,1024]{2,1,0:T(8,128)(2,1)}) custom-call(s32[8,128]{1,0:T(8,128)} %bitcast.3, bf16[4,80,1024]{2,1,0:T(8,128)(2,1)} %get-tuple-element.7.slices_hbm, bf16[4,80,768]{2,1,0:T(8,128)(2,1)} %get-tuple-element.8.factors_hbm, ...), custom_call_target="tpu_custom_call" | custom-call | tf_op jit(solution)/shard_map/pallas_call | solution.py:354

commit v5 on v4

--- a/solution.py
+++ b/solution.py
@@ -20,6 +20,10 @@
 
 def dot(a, b, ca=1, cb=0):
     return lax.dot_general(a, b, (((ca,), (cb,)), ((), ())), preferred_element_type=F32)
+
+
+def up_split(ff):
+    return ff // 3 * 2 if ff % 384 == 0 else ff
 
 
 def place(routes, owners):
@@ -168,10 +172,14 @@
     hidden = activated * up_pre
     gate_grad = hidden_grad * up_pre * sigmoid_gate * (1.0 + gate_pre * (1.0 - sigmoid_gate))
     up_grad = hidden_grad * activated
+    split = up_split(hidden.shape[1])
+    rest = hidden.shape[1] - split
+    beside = [hidden] + ([up_grad[:, split:]] if rest else [])
+    beside.append(jnp.zeros((slots, split - rest), F32))
     mine[...] = jnp.concatenate(
         [
-            jnp.concatenate([gate_grad, up_grad], axis=1),
-            jnp.concatenate([hidden, jnp.zeros_like(hidden)], axis=1),
+            jnp.concatenate([gate_grad, up_grad[:, :split]], axis=1),
+            jnp.concatenate(beside, axis=1),
         ],
         axis=0,
     ).astype(BF16)
@@ -286,7 +294,13 @@
     every = slices[...].reshape(many, part)
     top = lax.broadcasted_iota(jnp.int32, factors.shape, 1) < rows // 2
     held = factors[...].astype(F32)
-    value = jnp.where(top, held, 0.0).astype(BF16).reshape(many, 2 * ff)
+    value = jnp.where(top, held, 0.0)
+    rest = 2 * ff - held.shape[2]
+    if rest:
+        moved = held[:, rows // 2 :, ff : ff + rest]
+        moved = jnp.concatenate([moved, jnp.zeros_like(moved)], axis=1)
+        value = jnp.concatenate([value, moved], axis=2)
+    value = value.astype(BF16).reshape(many, 2 * ff)
     both = dot(every, value, 0, 0).astype(BF16)
     gate_grads[...] = both[:, :ff]
     up_grads[...] = both[:, ff:]
@@ -319,7 +333,7 @@
         functools.partial(kernel, groups, halves, owners),
         out_shape=(
             jax.ShapeDtypeStruct((groups, 2 * slots, part), BF16),
-            jax.ShapeDtypeStruct((groups, 2 * slots, 2 * ff), BF16),
+            jax.ShapeDtypeStruct((groups, 2 * slots, ff + up_split(ff)), BF16),
             jax.ShapeDtypeStruct((peers, ROWS, back_width), BF16),
         ),
         in_specs=[vmem] * 4 + [anywhere] * 3,
@@ -331,7 +345,7 @@
             pltpu.VMEM((owners, ROWS, width), BF16),
             pltpu.VMEM((peers, ROWS, width), BF16),
             pltpu.VMEM((2 * slots, model), BF16),
-            pltpu.VMEM((2 * slots, 2 * ff), BF16),
+            pltpu.VMEM((2 * slots, ff + up_split(ff)), BF16),
             pltpu.VMEM((peers, ROWS, back_width), BF16),
             dma((3,)),
             dma((peers,)),
@@ -363,7 +377,7 @@
         out_specs=(pl.BlockSpec(memory_space=pltpu.HBM),) * 4,
         scratch_shapes=[
             pltpu.VMEM((groups, 2 * slots, part), BF16),
-            pltpu.VMEM((groups, 2 * slots, 2 * ff), BF16),
+            pltpu.VMEM((groups, 2 * slots, ff + up_split(ff)), BF16),
             pltpu.VMEM((peers, ROWS, back_width), BF16),
             pltpu.VMEM((count, quarter), BF16),
             pltpu.VMEM((part, ff), BF16),

time: 41.2 us -> 40.2 us (0.976)
  Pallas kernels: 40.3 us -> 39.4 us
    pallas_call x1, Pallas kernels: 35.6 us -> 34.7 us  [local(): pl.pallas_call(functools.partial(kernel, groups, halves, owners), out_sha...]
where the time goes in v5:
time: 40.2 us; the launch traced here: 40 us
  Pallas kernels  39.4 us (98%)
  between operations  0.64 us (2%)
    pallas_call x1, Pallas kernels, local(): pl.pallas_call(functools.partial(kernel, groups, halves, owners), out_sha...  34.7 us
    pallas_call x1, Pallas kernels, local(): pl.pallas_call(functools.partial(finish, owners), out_shape=(jax.ShapeDty...  4.71 us

profile of v5, /device:TPU:8, one launch (start us, length us, event | category | flops | bytes accessed | tf_op | source)
XLA Modules:
  0.0 40.0 jit_solution(4652753896182000033)
XLA Ops:
  0.6 34.7 %shard_map.111 = (bf16[4,80,1024]{2,1,0:T(8,128)(2,1)}, bf16[4,80,640]{2,1,0:T(8,128)(2,1)}, bf16[8,80,256]{2,1,0:T(8,128)(2,1)}) custom-call(bf16[128,2048]{1,0:T(8,128)(2,1)} %tokens.1, bf16[128,2048]{1,0:T(8,128)(2,1)} %cotangent.1, s32[8,128]{1,0:T(8,128)} %bitcast.2, f32[8,128]{1,0:T(8,128)} %bitcast.4, bf16[1,4096,384]{2,1,0:T(8,128)(2,1)} %gate_hbm.1, ...), custom_call_target="tpu_custom_call" | custom-call | tf_op jit(solution)/shard_map/pallas_call | solution.py:332
  35.3 4.7 %shard_map.112 = (bf16[128,2048]{1,0:T(8,128)(2,1)}, bf16[1,1024,384]{2,1,0:T(8,128)(2,1)}, bf16[1,1024,384]{2,1,0:T(8,128)(2,1)}, bf16[1,384,1024]{2,1,0:T(8,128)(2,1)}) custom-call(s32[8,128]{1,0:T(8,128)} %bitcast.3, bf16[4,80,1024]{2,1,0:T(8,128)(2,1)} %get-tuple-element.7.slices_hbm, bf16[4,80,640]{2,1,0:T(8,128)(2,1)} %get-tuple-element.8.factors_hbm, ...), custom_call_target="tpu_custom_call" | custom-call | tf_op jit(solution)/shard_map/pallas_call | solution.py:368
